TPU v7x, 32 devices: a whole 2x2x4 slice. The times are simulated.
32 devices in a mesh: seq: 4 (over y, x), tensor: 8 (over z, core).
Axes of the slice: x: 2, y: 2, z: 4, core: 2. Of those that a mesh axis runs over, the one named last changes fastest.
Arguments:
- hidden_in: bfloat16 [4096, 2304], P(('seq', 'tensor')), may hold values from -6 to 6
- norm_attn: float32 [2304], replicated, may hold values from 0.1 to 1.9
- norm_ffn: float32 [2304], replicated, may hold values from 0.1 to 1.9
- w_qkv: bfloat16 [3, 2304, 512], P(None, None, 'tensor'), may hold values from -1 to 1
- w_out: bfloat16 [512, 2304], P('tensor'), may hold values from -0.25 to 0.25
- w_router: float32 [2304, 8], replicated, may hold values from -4 to 4
- w_gate_up: bfloat16 [2, 23040, 2304], P(None, 'tensor'), may hold values from -0.125 to 0.125
- w_down: bfloat16 [23040, 2304], P('tensor'), may hold values from -0.109375 to 0.109375
- segment_ids: int32 [4096], P('seq'), may hold values from 0 to 7, never falling along the last dimension, each value on 1 to 3072 neighbouring positions
- expert_ids: int32 [4096, 2], P(('seq', 'tensor')), may hold values from 0 to 7, all different within a row; in each aligned block of 128 rows (0 to 127, 128 to 255, ...) at most 64 rows name the same one
Outputs:
- hidden_out: bfloat16 [4096, 2304], P(('seq', 'tensor'))
- kv_cache: bfloat16 [8, 4096, 128], P('tensor', 'seq')
Inputs may be any that keep to these rules, and one draw needn't show every extreme that they name: `segment_ids`: nondecreasing along the stream; each prompt has 1 to 3072 tokens and one has exactly 3072. `expert_ids`: the two experts of a token differ. Within each aligned block of 128 tokens (the tokens of one device), no expert is named by more than 64 tokens, a bound that some block reaches.
All inputs are finite; a program needn't handle non-finite values.
Results may differ from a plain program's by a relative error of at most 0.019.
Values may be sent and summed in bfloat16 or wider, within the bound.
A program may use at most 128 MiB of HBM per device.

v0:
```python
import math
import jax
import jax.numpy as jnp
from jax import lax
from jax.sharding import PartitionSpec as P

HD = 64
epsilon = 1e-06
low_score = -1e30


def rms_norm(hidden_rows, gain):
    as_float = hidden_rows.astype(jnp.float32)
    scale = lax.rsqrt(jnp.mean(as_float * as_float, axis=-1, keepdims=True) + epsilon)
    return (as_float * scale * gain).astype(jnp.bfloat16)


def rotate(head_rows, positions):
    half_size = head_rows.shape[-1] // 2
    frequency = jnp.exp(jnp.arange(half_size, dtype=jnp.float32) * (-math.log(10000.0) / half_size))
    angles = positions.astype(jnp.float32)[:, None] * frequency[None, :]
    cosine = jnp.cos(angles)[:, None, :]
    sine_part = jnp.sin(angles)[:, None, :]
    front_half = head_rows[..., :half_size]
    back_half = head_rows[..., half_size:]
    return jnp.concatenate(
        [front_half * cosine - back_half * sine_part, back_half * cosine + front_half * sine_part],
        axis=-1,
    )


def fold_keys(
    softmax_state, query_rows, query_segments, query_positions, kv_rows, key_segments, key_start
):
    running_max, denominator, weighted_sum = softmax_state
    row_count = kv_rows.shape[0]
    block_size = math.gcd(row_count, 2048)
    head_size = query_rows.shape[-1]
    for block_start in range(0, row_count, block_size):
        kv_block = kv_rows[block_start : block_start + block_size]
        key_block = kv_block[..., :head_size]
        value_block = kv_block[..., head_size:]
        segment_block = key_segments[block_start : block_start + block_size]
        position_block = key_start + block_start + jnp.arange(block_size, dtype=jnp.int32)
        scores = (
            jnp.einsum("qhd,khd->hqk", query_rows, key_block, preferred_element_type=jnp.float32)
            * 0.125
        )
        allowed = (query_segments[:, None] == segment_block[None, :]) & (
            position_block[None, :] <= query_positions[:, None]
        )
        masked = jnp.where(allowed[None], scores, low_score)
        new_max = jnp.maximum(running_max, jnp.max(masked, axis=-1))
        weights = jnp.where(allowed[None], jnp.exp(masked - new_max[..., None]), 0.0)
        factor = jnp.exp(running_max - new_max)
        denominator = denominator * factor + jnp.sum(weights, axis=-1)
        weighted_sum = weighted_sum * factor[:, None, :] + jnp.einsum(
            "hqk,khd->hdq",
            weights.astype(jnp.bfloat16),
            value_block,
            preferred_element_type=jnp.float32,
        )
        running_max = new_max
    return (running_max, denominator, weighted_sum)


def pack_ids(ids, width):
    flat = ids.reshape(-1).astype(jnp.bfloat16)
    row_count = -(-flat.shape[0] // (16 * width)) * 16
    return jnp.pad(flat, (0, row_count * width - flat.shape[0])).reshape(row_count, width)


def unpack_ids(packed, count):
    row_count = -(-count // packed.shape[-1])
    used = packed[..., :row_count, :]
    return used.reshape(packed.shape[:-2] + (-1,))[..., :count].astype(jnp.int32)


def slot_table(token_ids, target, slot_count):
    is_routed = jnp.any(token_ids == target, axis=1).astype(jnp.int32)
    places = jnp.arange(is_routed.shape[0], dtype=jnp.int32)
    slot_rank = (
        jnp.sum(jnp.where(places[None, :] <= places[:, None], is_routed[None, :], 0), axis=1) - 1
    )
    chosen_slot = (is_routed[None, :] == 1) & (
        slot_rank[None, :] == jnp.arange(slot_count, dtype=jnp.int32)[:, None]
    )
    return chosen_slot.astype(jnp.bfloat16)


def expert_apply(slot_rows, slot_ids, own_expert, w_router, w_gate_up, w_down):
    logits = jnp.dot(slot_rows.astype(jnp.float32), w_router, precision=lax.Precision.HIGHEST)
    expert_count = w_router.shape[1]
    one_hot = (
        slot_ids[:, :, None] == jnp.arange(expert_count, dtype=jnp.int32)[None, None, :]
    ).astype(jnp.float32)
    chosen = jnp.sum(one_hot * logits[:, None, :], axis=-1)
    gate_probs = jax.nn.softmax(chosen, axis=-1)
    weight = jnp.sum(jnp.where(slot_ids == own_expert, gate_probs, 0.0), axis=-1)
    contract = (((1,), (1,)), ((), ()))
    gate_act = lax.dot_general(
        slot_rows, w_gate_up[0], contract, preferred_element_type=jnp.float32
    )
    up_act = lax.dot_general(slot_rows, w_gate_up[1], contract, preferred_element_type=jnp.float32)
    hidden_act = (jax.nn.silu(gate_act) * up_act).astype(jnp.bfloat16)
    output = jnp.dot(hidden_act, w_down, preferred_element_type=jnp.float32)
    return (output * weight[:, None]).astype(jnp.bfloat16)


def shards(
    hidden_in,
    norm_attn,
    norm_ffn,
    w_qkv,
    w_out,
    w_router,
    w_gate_up,
    w_down,
    segment_ids,
    expert_ids,
):
    local_rows = hidden_in.shape[0]
    model_width = hidden_in.shape[1]
    tensor_count = lax.axis_size("tensor")
    tensor_place = lax.axis_index("tensor")
    seq_place = lax.axis_index("seq")
    group_rows = local_rows * tensor_count
    head_count = w_qkv.shape[2] // HD
    full_hidden = lax.all_gather(hidden_in, "tensor", axis=0, tiled=True)
    projected = jnp.einsum(
        "td,cdh->tch", rms_norm(full_hidden, norm_attn), w_qkv, preferred_element_type=jnp.float32
    )
    positions = seq_place * group_rows + jnp.arange(group_rows, dtype=jnp.int32)
    query_rows = rotate(projected[:, 0].reshape(group_rows, head_count, HD), positions).astype(
        jnp.bfloat16
    )
    key_rows = rotate(projected[:, 1].reshape(group_rows, head_count, HD), positions).astype(
        jnp.bfloat16
    )
    value_rows = projected[:, 2].reshape(group_rows, head_count, HD).astype(jnp.bfloat16)
    kv_rows = jnp.concatenate([key_rows, value_rows], axis=-1)
    kv_cache = kv_rows.transpose(1, 0, 2)
    seq_count = lax.axis_size("seq")
    kv_flat = kv_cache.reshape(head_count * group_rows, 2 * HD)
    kv_packed = jnp.concatenate([kv_flat, pack_ids(segment_ids, 2 * HD)], axis=0)
    out_packed = jnp.concatenate([w_out, pack_ids(expert_ids, model_width)], axis=0)
    kv_packed, out_packed = lax.optimization_barrier((kv_packed, out_packed))
    arrivals = []
    for step in range(1, seq_count):
        pairs = [(i, i ^ step) for i in range(seq_count)]
        arrivals.append((lax.ppermute(kv_packed, "seq", pairs), seq_place ^ step))
    out_gathered = lax.all_gather(out_packed, "tensor", axis=0)
    full_ids = unpack_ids(out_gathered[:, w_out.shape[0] :], 2 * local_rows)
    w_out_full = out_gathered[:, : w_out.shape[0]].reshape(-1, model_width)
    start_state = (
        jnp.full((head_count, group_rows), low_score, jnp.float32),
        jnp.zeros((head_count, group_rows), jnp.float32),
        jnp.zeros((head_count, HD, group_rows), jnp.float32),
    )
    softmax_state = fold_keys(
        start_state,
        query_rows,
        segment_ids,
        positions,
        kv_rows,
        segment_ids,
        seq_place * group_rows,
    )
    for arrived, source in arrivals:
        softmax_state = fold_keys(
            softmax_state,
            query_rows,
            segment_ids,
            positions,
            arrived[: kv_flat.shape[0]].reshape(head_count, group_rows, 2 * HD).transpose(1, 0, 2),
            unpack_ids(arrived[kv_flat.shape[0] :], group_rows),
            source * group_rows,
        )
    running_max, denominator, weighted_sum = softmax_state
    attended = (
        (weighted_sum / denominator[:, None, :])
        .astype(jnp.bfloat16)
        .reshape(head_count * HD, group_rows)
    )
    attended, w_out_full = lax.optimization_barrier((attended, w_out_full))
    attention_sum = lax.dot_general(
        lax.all_gather(attended, "tensor", axis=0, tiled=True),
        w_out_full,
        (((0,), (0,)), ((), ())),
        preferred_element_type=jnp.float32,
    )
    full_residual = full_hidden.astype(jnp.float32) + attention_sum
    full_rows = rms_norm(full_residual, norm_ffn)
    residual = lax.dynamic_slice_in_dim(full_residual, tensor_place * local_rows, local_rows, 0)
    expert_count = w_router.shape[1]
    slice_count = tensor_count // expert_count
    own_expert = tensor_place // slice_count
    slot_count = local_rows // 2
    block_ids = full_ids.reshape(tensor_count, local_rows, 2)
    slot_tables = jax.vmap(lambda source_ids: slot_table(source_ids, own_expert, slot_count))(
        block_ids
    )
    slot_rows = jnp.einsum(
        "sjr,srd->sjd",
        slot_tables,
        full_rows.reshape(tensor_count, local_rows, model_width),
        preferred_element_type=jnp.float32,
    ).astype(jnp.bfloat16)
    slot_ids = jnp.einsum(
        "sjr,srk->sjk", slot_tables.astype(jnp.float32), block_ids.astype(jnp.float32)
    ).astype(jnp.int32)
    term_rows = expert_apply(
        slot_rows.reshape(-1, model_width),
        slot_ids.reshape(-1, 2),
        own_expert,
        w_router,
        w_gate_up,
        w_down,
    )
    placed = jnp.einsum(
        "sjr,sjd->srd",
        slot_tables,
        term_rows.reshape(tensor_count, slot_count, model_width),
        preferred_element_type=jnp.float32,
    ).reshape(group_rows, model_width)
    expert_sum = lax.psum_scatter(
        placed.astype(jnp.bfloat16), "tensor", scatter_dimension=0, tiled=True
    ).astype(jnp.float32)
    hidden_out = (residual + expert_sum).astype(jnp.bfloat16)
    return (hidden_out, kv_cache)


def solution(mesh):
    placed = (
        P(("seq", "tensor"), None),
        P(),
        P(),
        P(None, None, "tensor"),
        P("tensor", None),
        P(),
        P(None, "tensor", None),
        P("tensor", None),
        P("seq"),
        P(("seq", "tensor"), None),
    )
    return jax.shard_map(
        shards,
        mesh=mesh,
        in_specs=placed,
        out_specs=(P(("seq", "tensor"), None), P("tensor", "seq", None)),
        check_vma=False,
    )
```

profile of v0, /device:TPU:0, one launch (start us, length us, event | category | flops | bytes accessed | tf_op | source)
XLA Modules:
  0.0 253.3 jit_solution(6927243527488938776)
XLA Ops:
  9.9 1.7 pad_maximum_fusion
  11.6 52.5 %all-gather.5.cloned.1.call-done = bf16[1024,2304]{1,0:T(8,128)(2,1)} async-done(((bf16[128,2304]{1,0:T(8,128)(2,1)}), bf16[1024,2304]{1,0:T(8,128)(2,1)}) %all-gather.5.cloned.1.call-update) | async-done | bytes 4718608 | tf_op jit(solution)/shard_map/all_gather | solution.py:129
  64.1 3.5 %fusion.6 = f32[1024]{0:T(1024)S(1)} fusion(bf16[1024,2304]{1,0:T(8,128)(2,1)} %all-gather.5.cloned.1.call-done), kind=kLoop, calls=%fused_computation.9 | loop fusion | flops 7076864 | bytes 4722688 | tf_op jit(solution)/shard_map/reduce_sum | solution.py:14
  67.9 1.8 fusion.11
  70.8 3.1 %fusion.76 = (bf16[1024,1,32]{2,0,1:T(8,128)(2,1)S(1)}, bf16[1024,1,32]{2,0,1:T(8,128)(2,1)S(1)}, bf16[1024,32]{1,0:T(8,128)(2,1)S(1)}, bf16[1024,32]{1,0:T(8,128)(2,1)}) fusion(f32[1024,1,32]{2,0,1:T(8,128)S(1)} %copy.84, f32[1024,1,32]{2,0,1:T(8,128)S(1)} %copy.83, f32[32]{0:T(128)S(1)} %multiply_exponential_fusion, f32[1024]{0:T(1024)S(1)} %fusion.107, ...), kind=kLoop, calls=%fused_computation.76 | loop fusion | flops 557056 | bytes 790656 | tf_op jit(solution)/shard_map/convert.9
  73.9 1.0 fusion.124
  74.9 1.5 collective-permute-start
  76.4 1.5 collective-permute-start.1
  78.8 1.1 pad_maximum_fusion.2
  80.7 3.5 %collective-permute-done = bf16[1040,128]{1,0:T(8,128)(2,1)S(1)} collective-permute-done((bf16[1040,128]{1,0:T(8,128)(2,1)S(1)}, bf16[1040,128]{1,0:T(8,128)(2,1)S(1)}, u32[]{:S(2)}, u32[]{:S(2)}) %collective-permute-start) | collective-permute-done | bytes 266272 | tf_op jit(solution)/shard_map/ppermute | solution.py:151
  84.9 5.5 %collective-permute-done.1 = bf16[1040,128]{1,0:T(8,128)(2,1)S(1)} collective-permute-done((bf16[1040,128]{1,0:T(8,128)(2,1)S(1)}, bf16[1040,128]{1,0:T(8,128)(2,1)S(1)}, u32[]{:S(2)}, u32[]{:S(2)}) %collective-permute-start.1) | collective-permute-done | bytes 266272 | tf_op jit(solution)/shard_map/ppermute | solution.py:151
  90.4 3.2 %fusion.18 = (f32[1024]{0:T(1024)S(1)}, f32[1024]{0:T(1024)S(1)}, f32[1024]{0:T(1024)S(1)}, f32[1024,1024]{0,1:T(8,128)S(1)}) fusion(s32[1024]{0:T(1024)S(1)} %get-tuple-element.56, s32[1024]{0:T(1024)S(1)} %copy-done.5, s32[1024]{0:T(1024)S(1)} %get-tuple-element.58, s32[1024]{0:T(1024)S(1)} %fusion.105, f32[1024,1024]{0,1:T(8,128)S(1)} %fusion.84, ...), kind=kOutput, calls=%fused_computation.36 | convolution fusion | flops 153089024 | bytes 13152256 | tf_op jit(solution)/shard_map/qhd,khd->hqk/dot_general | solution.py:46
  93.6 5.9 %fusion.20 = (f32[1024]{0:T(1024)S(1)}, f32[1024]{0:T(1024)S(1)}, f32[1024]{0:T(1024)S(1)}, f32[1024]{0:T(1024)S(1)}, f32[1024,1024]{0,1:T(8,128)S(1)}) fusion(f32[1024,1024]{0,1:T(8,128)S(1)} %fusion.84, f32[1024]{0:T(1024)S(1)} %get-tuple-element.46, s32[1024]{0:T(1024)S(1)} %get-tuple-element.56, s32[1024]{0:T(1024)S(1)} %copy-done.5, ...), kind=kOutput, calls=%fused_computation.38 | convolution fusion | flops 165670912 | bytes 17371136 | tf_op jit(solution)/shard_map/qhd,khd->hqk/dot_general | solution.py:46
  99.5 2.1 fusion.26
  101.7 1.8 fusion.32
  103.5 1.8 fusion.30
  105.3 1.4 fusion.54
  106.6 2.2 fusion.60
  108.9 5.2 %all-gather.9.cloned.1.call-done = bf16[640,2304]{1,0:T(8,128)(2,1)} async-done(((bf16[80,2304]{1,0:T(8,128)(2,1)}), bf16[640,2304]{1,0:T(8,128)(2,1)}) %all-gather.9.cloned.1.call-update) | async-done | bytes 2949136 | tf_op jit(solution)/shard_map/all_gather | solution.py:152
  114.1 1.8 slice.120
  116.2 1.0 slice.121
  118.5 18.6 %all-gather.7.cloned.1.call-done = bf16[512,1024]{1,0:T(8,128)(2,1)} async-done(((bf16[64,1024]{1,0:T(8,128)(2,1)}), bf16[512,1024]{1,0:T(8,128)(2,1)}) %all-gather.7.cloned.1.call-update) | async-done | bytes 1048592 | tf_op jit(solution)/shard_map/all_gather | solution.py:187
  137.1 6.1 %multiply_reduce_fusion = (f32[1024]{0:T(1024)S(1)}, f32[1024,2304]{1,0:T(8,128)S(1)}) fusion(bf16[512,1024]{1,0:T(8,128)(2,1)} %all-gather.7.cloned.1.call-done, bf16[512,2304]{1,0:T(8,128)(2,1)S(1)} %bitcast.110, bf16[1024,2304]{1,0:T(8,128)(2,1)} %all-gather.5.cloned.1.call-done), kind=kOutput, calls=%fused_computation.13 | convolution fusion | flops 2425355264 | bytes 17567744 | tf_op jit(solution)/shard_map/dot_general | solution.py:186
  143.2 0.9 multiply_convert_fusion
  144.1 2.7 %copy-done.2 = f32[1024,2304]{1,0:T(8,128)} copy-done((f32[1024,2304]{1,0:T(8,128)}, f32[1024,2304]{1,0:T(8,128)S(1)}, u32[]{:S(2)}) %copy-start.2) | copy-done | bytes 9437208
  146.8 0.8 convolution_convert_fusion.1
  147.7 1.9 fusion.129
  149.8 12.0 %fusion.2 = f32[512,2880]{0,1:T(8,128)} fusion(bf16[512,2304]{1,0:T(8,128)(2,1)S(1)} %bitcast.107, bf16[2,2880,2304]{2,1,0:T(8,128)(2,1)} %param.16), kind=kOutput, calls=%fused_computation.5 | convolution fusion | flops 6794772480 | bytes 21528576 | tf_op jit(solution)/shard_map/dot_general | solution.py:101
  162.0 22.0 %fusion.15 = bf16[512,2304]{1,0:T(8,128)(2,1)} fusion(bf16[2880,2304]{1,0:T(8,128)(2,1)} %param.17, f32[512]{0:T(512)S(1)} %mul.262, f32[512,2880]{0,1:T(8,128)} %fusion.2, bf16[512,2304]{1,0:T(8,128)(2,1)S(1)} %bitcast.108, bf16[2,2880,2304]{2,1,0:T(8,128)(2,1)} %param.16), kind=kOutput, calls=%fused_computation.21 | convolution fusion | flops 13600751616 | bytes 37160960 | tf_op jit(solution)/shard_map/dot_general | solution.py:106
  184.0 5.4 %convolution_convert_fusion = bf16[8,128,2304]{2,1,0:T(8,128)(2,1)} fusion(bf16[8,64,2304]{2,1,0:T(8,128)(2,1)} %bitcast.109, s32[8,128]{1,0:T(8,128)S(1)} %broadcast_add_fusion, pred[8,128]{1,0:T(8,128)(4,1)S(1)} %get-tuple-element.47), kind=kOutput, calls=%fused_computation.15 | convolution fusion | flops 304480256 | bytes 7083008 | tf_op jit(solution)/shard_map/sjr,sjd->srd/dot_general | solution.py:220
  189.4 54.7 %reduce-scatter.2.cloned.1.call-done = bf16[128,2304]{1,0:T(8,128)(2,1)} async-done(((bf16[1024,2304]{1,0:T(8,128)(2,1)}), bf16[128,2304]{1,0:T(8,128)(2,1)}) %reduce-scatter.2.cloned.1.call-update) | async-done | bytes 589840 | tf_op jit(solution)/shard_map/reduce_scatter | solution.py:226
  244.1 2.4 add_convert_fusion
  (81 shorter events, 8.4 us)
Async XLA Ops:
  7.2 60.4 %copy-start = (bf16[3,2304,64]{1,2,0:T(8,128)(2,1)S(1)}, bf16[3,2304,64]{1,2,0:T(8,128)(2,1)}, u32[]{:S(2)}) copy-start(bf16[3,2304,64]{1,2,0:T(8,128)(2,1)} %param.13) | copy-start | bytes 2654212
  7.2 60.4 %copy-start.7 = (f32[2304]{0:T(1024)S(1)}, f32[2304]{0:T(1024)}, u32[]{:S(2)}) copy-start(f32[2304]{0:T(1024)} %param.11) | copy-start | bytes 27652
  7.2 56.9 %all-gather.5.cloned.1.call-start = ((), (), s32[]{:S(2)}) async-start(), calls=%async_computation.1 | async-start | bytes 5308416 | tf_op jit(solution)/shard_map/all_gather | solution.py:129
  7.9 106.1 %all-gather.9.cloned.1.call-start = ((), (), s32[]{:S(2)}) async-start(), calls=%async_computation.4 | async-start | bytes 3317760 | tf_op jit(solution)/shard_map/all_gather | solution.py:152
  64.1 3.8 %copy-start.3 = (bf16[1024,2304]{1,0:T(8,128)(2,1)S(1)}, bf16[1024,2304]{1,0:T(8,128)(2,1)}, u32[]{:S(2)}) copy-start(bf16[1024,2304]{1,0:T(8,128)(2,1)} %all-gather.5.cloned.1.call-done) | copy-start | bytes 14155780
  74.9 9.3 %collective-permute-start = (bf16[1040,128]{1,0:T(8,128)(2,1)S(1)}, bf16[1040,128]{1,0:T(8,128)(2,1)S(1)}, u32[]{:S(2)}, u32[]{:S(2)}) collective-permute-start(bf16[1040,128]{1,0:T(8,128)(2,1)S(1)} %pad_maximum_fusion.1), channel_id=1, source_target_pairs={{0,8},{8,0},{16,24},{24,16},{1,9},{9,1},{17,25},{25,17},{2,10},{10... | collective-permute-start | bytes 798728 | tf_op jit(solution)/shard_map/ppermute | solution.py:151
  76.4 14.0 %collective-permute-start.1 = (bf16[1040,128]{1,0:T(8,128)(2,1)S(1)}, bf16[1040,128]{1,0:T(8,128)(2,1)S(1)}, u32[]{:S(2)}, u32[]{:S(2)}) collective-permute-start(bf16[1040,128]{1,0:T(8,128)(2,1)S(1)} %pad_maximum_fusion.1), channel_id=1, source_target_pairs={{0,16},{8,24},{16,0},{24,8},{1,17},{9,25},{17,1},{25,9},{2,18},{10... | collective-permute-start | bytes 798728 | tf_op jit(solution)/shard_map/ppermute | solution.py:151
  77.9 15.7 %collective-permute-start.2 = (bf16[1040,128]{1,0:T(8,128)(2,1)S(1)}, bf16[1040,128]{1,0:T(8,128)(2,1)S(1)}, u32[]{:S(2)}, u32[]{:S(2)}) collective-permute-start(bf16[1040,128]{1,0:T(8,128)(2,1)S(1)} %pad_maximum_fusion.1), channel_id=1, source_target_pairs={{0,24},{8,16},{16,8},{24,0},{1,25},{9,17},{17,9},{25,1},{2,26},{10... | collective-permute-start | bytes 798728 | tf_op jit(solution)/shard_map/ppermute | solution.py:151
  78.4 58.6 %all-gather.7.cloned.1.call-start = ((), (), s32[]{:S(2)}) async-start(), calls=%async_computation.2 | async-start | bytes 1179648 | tf_op jit(solution)/shard_map/all_gather | solution.py:187
  79.9 10.5 %copy-start.5 = (s32[1024]{0:T(1024)S(1)}, s32[1024]{0:T(1024)}, u32[]{:S(2)}) copy-start(s32[1024]{0:T(1024)} %param.18) | copy-start | bytes 12292
  115.9 128.2 %reduce-scatter.2.cloned.1.call-start = ((), (), s32[]{:S(2)}) async-start(), calls=%async_computation.3 | async-start | bytes 5308416 | tf_op jit(solution)/shard_map/reduce_scatter | solution.py:226
  118.5 24.7 %copy-start.6 = (f32[2304]{0:T(1024)S(1)}, f32[2304]{0:T(1024)}, u32[]{:S(2)}) copy-start(f32[2304]{0:T(1024)} %param.12) | copy-start | bytes 27652
  143.2 3.6 %copy-start.2 = (f32[1024,2304]{1,0:T(8,128)}, f32[1024,2304]{1,0:T(8,128)S(1)}, u32[]{:S(2)}) copy-start(f32[1024,2304]{1,0:T(8,128)S(1)} %get-tuple-element.52) | copy-start | bytes 28311556
  146.8 0.9 copy-start.4
  184.0 62.5 %copy-start.1 = (bf16[3,2304,64]{1,2,0:T(8,128)(2,1)S(1)}, bf16[3,2304,64]{1,2,0:T(8,128)(2,1)}, u32[]{:S(2)}) copy-start(bf16[3,2304,64]{1,2,0:T(8,128)(2,1)} %param.13) | copy-start | bytes 2654212
Sparse Core Ops, SparseCore 0:
  9.7 54.3 all-gather.4
  78.6 35.4 all-gather.8
  116.1 20.9 all-gather.6
  189.5 54.5 reduce-scatter.1
where the time goes:
time: 257 us; the launch traced here: 253 us
  waiting for transfers between devices  141 us (55%)
  matrix products  67.8 us (26%)
  other arithmetic  17.8 us (7%)
  between operations  14.4 us (6%)
  local copies, waits for them, and re-layouts  8.32 us (3%)
  starting transfers between devices  4.18 us (2%)
    reduce_scatter x1, waiting for transfers between devices, shards(): lax.psum_scatter(placed.astype(jnp.bfloat16), 'tensor', scatter_dimension...  54.7 us
    all_gather x1, waiting for transfers between devices, shards(): full_hidden = lax.all_gather(hidden_in, 'tensor', axis=0, tiled=True)  52.5 us
    dot_general x1, matrix products, expert_apply(): output = jnp.dot(hidden_act, w_down, preferred_element_type=jnp.float32)  22 us
    all_gather x1, waiting for transfers between devices, shards(): lax.all_gather(attended, 'tensor', axis=0, tiled=True)  18.6 us
    dot_general x1, matrix products, expert_apply(): lax.dot_general(slot_rows, w_gate_up[0], contract, preferred_element_type...  12 us
    dot_general x4, matrix products, fold_keys(): jnp.einsum('qhd,khd->hqk', query_rows, key_block, preferred_element_type=...  10.5 us
    ppermute x3, waiting for transfers between devices, shards(): arrivals.append((lax.ppermute(kv_packed, 'seq', pairs), seq_place ^ step))  8.96 us
    dot_general x4, matrix products, fold_keys(): jnp.einsum('hqk,khd->hdq', weights.astype(jnp.bfloat16), value_block, pre...  7.18 us
  transfers between devices with their start and end apart: 7, of which 6 were waited for; matrix products, arithmetic and copies ran while one was open for 11% of the time, Pallas kernels for 0%

commit v1 on v0

--- a/solution.py
+++ b/solution.py
@@ -126,7 +126,14 @@
     seq_place = lax.axis_index("seq")
     group_rows = local_rows * tensor_count
     head_count = w_qkv.shape[2] // HD
-    full_hidden = lax.all_gather(hidden_in, "tensor", axis=0, tiled=True)
+    ring = [hidden_in]
+    for hop in range(7):
+        ring.append(lax.ppermute(ring[-1], "tensor", [(dev, (dev + 1) % 8) for dev in range(8)]))
+    full_hidden = jnp.roll(
+        jnp.concatenate(ring[::-1], axis=0),
+        (lax.axis_index("tensor") + 1) * ring[0].shape[0],
+        axis=0,
+    )
     projected = jnp.einsum(
         "td,cdh->tch", rms_norm(full_hidden, norm_attn), w_qkv, preferred_element_type=jnp.float32
     )

time: 257 us -> 287 us (1.12)
  waiting for transfers between devices: 141 us -> 163 us
  local copies, waits for them, and re-layouts: 8.32 us -> 16.7 us
    ppermute x0 -> x7, waiting for transfers between devices: none -> 75.2 us  [shards(): lax.ppermute(ring[-1], 'tensor', [(dev, (dev + 1) % 8) for dev in range(8)])]
    all_gather x1 -> x0, waiting for transfers between devices: 52.5 us -> none  [shards(): full_hidden = lax.all_gather(hidden_in, 'tensor', axis=0, tiled=True)]
    unnamed x22 -> x47, local copies, waits for them, and re-layouts: 4.05 us -> 12.4 us
    ppermute x3, waiting for transfers between devices: 8.96 us -> 4.75 us  [shards(): arrivals.append((lax.ppermute(kv_packed, 'seq', pairs), seq_place ^ step))]
    all_gather x1, waiting for transfers between devices: 5.21 us -> 9.26 us  [shards(): out_gathered = lax.all_gather(out_packed, 'tensor', axis=0)]
  transfers between devices with their start and end apart: 7 -> 13, of which waited for: 6 -> 12; matrix products, arithmetic and copies ran while one was open for 11% -> 10% of each run, Pallas kernels for 0% -> 0%
where the time goes in v1:
time: 287 us; the launch traced here: 282 us
  waiting for transfers between devices  163 us (57%)
  matrix products  67.8 us (24%)
  local copies, waits for them, and re-layouts  16.7 us (6%)
  other arithmetic  15.3 us (5%)
  between operations  14.5 us (5%)
  starting transfers between devices  4.7 us (2%)
    ppermute x7, waiting for transfers between devices, shards(): lax.ppermute(ring[-1], 'tensor', [(dev, (dev + 1) % 8) for dev in range(8)])  75.2 us
    reduce_scatter x1, waiting for transfers between devices, shards(): lax.psum_scatter(placed.astype(jnp.bfloat16), 'tensor', scatter_dimension...  54.7 us
    dot_general x1, matrix products, expert_apply(): output = jnp.dot(hidden_act, w_down, preferred_element_type=jnp.float32)  22 us
    all_gather x1, waiting for transfers between devices, shards(): lax.all_gather(attended, 'tensor', axis=0, tiled=True)  18.7 us
    unnamed x47, local copies, waits for them, and re-layouts  12.4 us
    dot_general x1, matrix products, expert_apply(): lax.dot_general(slot_rows, w_gate_up[0], contract, preferred_element_type...  12 us
    dot_general x4, matrix products, fold_keys(): jnp.einsum('qhd,khd->hqk', query_rows, key_block, preferred_element_type=...  10.5 us
    all_gather x1, waiting for transfers between devices, shards(): out_gathered = lax.all_gather(out_packed, 'tensor', axis=0)  9.26 us
  transfers between devices with their start and end apart: 13, of which 12 were waited for; matrix products, arithmetic and copies ran while one was open for 10% of the time, Pallas kernels for 0%

profile of v1, /device:TPU:0, one launch (start us, length us, event | category | flops | bytes accessed | tf_op | source)
XLA Modules:
  0.0 281.9 jit_solution(2378951050063338345)
XLA Ops:
  7.7 11.8 %collective-permute-done = bf16[128,2304]{1,0:T(8,128)(2,1)S(1)} collective-permute-done((bf16[128,2304]{1,0:T(8,128)(2,1)}, bf16[128,2304]{1,0:T(8,128)(2,1)S(1)}, u32[]{:S(2)}, u32[]{:S(2)}) %collective-permute-start) | collective-permute-done | bytes 589856 | tf_op jit(solution)/shard_map/ppermute | solution.py:131
  19.6 11.1 %collective-permute-done.1 = bf16[128,2304]{1,0:T(8,128)(2,1)S(1)} collective-permute-done((bf16[128,2304]{1,0:T(8,128)(2,1)S(1)}, bf16[128,2304]{1,0:T(8,128)(2,1)S(1)}, u32[]{:S(2)}, u32[]{:S(2)}) %collective-permute-start.1) | collective-permute-done | bytes 589856 | tf_op jit(solution)/shard_map/ppermute | solution.py:131
  30.7 11.1 %collective-permute-done.2 = bf16[128,2304]{1,0:T(8,128)(2,1)S(1)} collective-permute-done((bf16[128,2304]{1,0:T(8,128)(2,1)S(1)}, bf16[128,2304]{1,0:T(8,128)(2,1)S(1)}, u32[]{:S(2)}, u32[]{:S(2)}) %collective-permute-start.2) | collective-permute-done | bytes 589856 | tf_op jit(solution)/shard_map/ppermute | solution.py:131
  41.8 11.1 %collective-permute-done.3 = bf16[128,2304]{1,0:T(8,128)(2,1)S(1)} collective-permute-done((bf16[128,2304]{1,0:T(8,128)(2,1)S(1)}, bf16[128,2304]{1,0:T(8,128)(2,1)S(1)}, u32[]{:S(2)}, u32[]{:S(2)}) %collective-permute-start.3) | collective-permute-done | bytes 589856 | tf_op jit(solution)/shard_map/ppermute | solution.py:131
  53.7 11.1 %collective-permute-done.4 = bf16[128,2304]{1,0:T(8,128)(2,1)S(1)} collective-permute-done((bf16[128,2304]{1,0:T(8,128)(2,1)S(1)}, bf16[128,2304]{1,0:T(8,128)(2,1)S(1)}, u32[]{:S(2)}, u32[]{:S(2)}) %collective-permute-start.4) | collective-permute-done | bytes 589856 | tf_op jit(solution)/shard_map/ppermute | solution.py:131
  65.5 10.5 %collective-permute-done.5 = bf16[128,2304]{1,0:T(8,128)(2,1)} collective-permute-done((bf16[128,2304]{1,0:T(8,128)(2,1)S(1)}, bf16[128,2304]{1,0:T(8,128)(2,1)}, u32[]{:S(2)}, u32[]{:S(2)}) %collective-permute-start.5) | collective-permute-done | bytes 589856 | tf_op jit(solution)/shard_map/ppermute | solution.py:131
  77.2 1.7 pad_maximum_fusion
  78.9 8.5 %collective-permute-done.6 = bf16[128,2304]{1,0:T(8,128)(2,1)} collective-permute-done((bf16[128,2304]{1,0:T(8,128)(2,1)}, bf16[128,2304]{1,0:T(8,128)(2,1)}, u32[]{:S(2)}, u32[]{:S(2)}) %collective-permute-start.6) | collective-permute-done | bytes 589856 | tf_op jit(solution)/shard_map/ppermute | solution.py:131
  90.8 1.2 constant_dynamic-update-slice_fusion.12
  95.7 1.8 fusion.11
  99.4 3.1 %fusion.77 = (bf16[1024,1,32]{2,0,1:T(8,128)(2,1)S(1)}, bf16[1024,1,32]{2,0,1:T(8,128)(2,1)S(1)}, bf16[1024,32]{1,0:T(8,128)(2,1)S(1)}, bf16[1024,32]{1,0:T(8,128)(2,1)}) fusion(f32[1024,1,32]{2,0,1:T(8,128)S(1)} %copy.84, f32[1024,1,32]{2,0,1:T(8,128)S(1)} %copy.83, f32[32]{0:T(128)S(1)} %multiply_exponential_fusion, f32[1024]{0:T(1024)S(1)} %fusion.108, ...), kind=kLoop, calls=%fused_computation.77 | loop fusion | flops 557056 | bytes 790656 | tf_op jit(solution)/shard_map/convert.9
  103.5 2.1 collective-permute-start.7
  105.5 1.5 collective-permute-start.8
  110.7 4.1 %collective-permute-done.8 = bf16[1040,128]{1,0:T(8,128)(2,1)S(1)} collective-permute-done((bf16[1040,128]{1,0:T(8,128)(2,1)S(1)}, bf16[1040,128]{1,0:T(8,128)(2,1)S(1)}, u32[]{:S(2)}, u32[]{:S(2)}) %collective-permute-start.8) | collective-permute-done | bytes 266272 | tf_op jit(solution)/shard_map/ppermute | solution.py:158
  114.8 3.2 %fusion.18 = (f32[1024]{0:T(1024)S(1)}, f32[1024]{0:T(1024)S(1)}, f32[1024]{0:T(1024)S(1)}, f32[1024,1024]{0,1:T(8,128)S(1)}) fusion(s32[1024]{0:T(1024)S(1)} %get-tuple-element.56, s32[1024]{0:T(1024)S(1)} %copy-done.10, s32[1024]{0:T(1024)S(1)} %get-tuple-element.58, s32[1024]{0:T(1024)S(1)} %fusion.106, f32[1024,1024]{0,1:T(8,128)S(1)} %fusion.85, ...), kind=kOutput, calls=%fused_computation.36 | convolution fusion | flops 153089024 | bytes 13152256 | tf_op jit(solution)/shard_map/qhd,khd->hqk/dot_general | solution.py:46
  118.1 5.9 %fusion.21 = (f32[1024]{0:T(1024)S(1)}, f32[1024]{0:T(1024)S(1)}, f32[1024]{0:T(1024)S(1)}, f32[1024]{0:T(1024)S(1)}, f32[1024,1024]{0,1:T(8,128)S(1)}) fusion(f32[1024,1024]{0,1:T(8,128)S(1)} %fusion.85, f32[1024]{0:T(1024)S(1)} %get-tuple-element.46, s32[1024]{0:T(1024)S(1)} %get-tuple-element.56, s32[1024]{0:T(1024)S(1)} %copy-done.10, ...), kind=kOutput, calls=%fused_computation.39 | convolution fusion | flops 165670912 | bytes 17371136 | tf_op jit(solution)/shard_map/qhd,khd->hqk/dot_general | solution.py:46
  124.0 2.1 fusion.27
  126.1 1.8 fusion.33
  127.9 1.8 fusion.31
  129.7 1.4 fusion.55
  131.1 2.2 fusion.61
  133.3 9.3 %all-gather.6.cloned.1.call-done = bf16[640,2304]{1,0:T(8,128)(2,1)} async-done(((bf16[80,2304]{1,0:T(8,128)(2,1)}), bf16[640,2304]{1,0:T(8,128)(2,1)}) %all-gather.6.cloned.1.call-update) | async-done | bytes 2949136 | tf_op jit(solution)/shard_map/all_gather | solution.py:159
  142.6 1.8 slice.120
  147.0 18.7 %all-gather.4.cloned.1.call-done = bf16[512,1024]{1,0:T(8,128)(2,1)} async-done(((bf16[64,1024]{1,0:T(8,128)(2,1)}), bf16[512,1024]{1,0:T(8,128)(2,1)}) %all-gather.4.cloned.1.call-update) | async-done | bytes 1048592 | tf_op jit(solution)/shard_map/all_gather | solution.py:194
  165.8 6.1 %multiply_reduce_fusion = (f32[1024]{0:T(1024)S(1)}, f32[1024,2304]{1,0:T(8,128)S(1)}) fusion(bf16[512,1024]{1,0:T(8,128)(2,1)} %all-gather.4.cloned.1.call-done, bf16[512,2304]{1,0:T(8,128)(2,1)S(1)} %bitcast.110, bf16[2048,2304]{1,0:T(8,128)(2,1)} %copy-done.3, s32[]{:T(128)S(6)} %select_n.61), kind=kOutput, calls=%fused_computation.13 | convolution fusion | flops 2425355264 | bytes 17567748 | tf_op jit(solution)/shard_map/dot_general | solution.py:193
  172.8 2.7 copy-done.2
  176.3 1.9 fusion.131
  178.5 12.0 %fusion.2 = f32[512,2880]{0,1:T(8,128)} fusion(bf16[512,2304]{1,0:T(8,128)(2,1)S(1)} %bitcast.107, bf16[2,2880,2304]{2,1,0:T(8,128)(2,1)} %param.16), kind=kOutput, calls=%fused_computation.5 | convolution fusion | flops 6794772480 | bytes 21528576 | tf_op jit(solution)/shard_map/dot_general | solution.py:101
  190.7 22.0 %fusion.15 = bf16[512,2304]{1,0:T(8,128)(2,1)} fusion(bf16[2880,2304]{1,0:T(8,128)(2,1)} %param.17, f32[512]{0:T(512)S(1)} %mul.266, f32[512,2880]{0,1:T(8,128)} %fusion.2, bf16[512,2304]{1,0:T(8,128)(2,1)S(1)} %bitcast.108, bf16[2,2880,2304]{2,1,0:T(8,128)(2,1)} %param.16), kind=kOutput, calls=%fused_computation.21 | convolution fusion | flops 13600751616 | bytes 37160960 | tf_op jit(solution)/shard_map/dot_general | solution.py:106
  212.6 5.4 %convolution_convert_fusion = bf16[8,128,2304]{2,1,0:T(8,128)(2,1)} fusion(bf16[8,64,2304]{2,1,0:T(8,128)(2,1)} %bitcast.109, s32[8,128]{1,0:T(8,128)S(1)} %broadcast_add_fusion, pred[8,128]{1,0:T(8,128)(4,1)S(1)} %get-tuple-element.47), kind=kOutput, calls=%fused_computation.15 | convolution fusion | flops 304480256 | bytes 7083008 | tf_op jit(solution)/shard_map/sjr,sjd->srd/dot_general | solution.py:227
  218.1 54.7 %reduce-scatter.2.cloned.1.call-done = bf16[128,2304]{1,0:T(8,128)(2,1)} async-done(((bf16[1024,2304]{1,0:T(8,128)(2,1)}), bf16[128,2304]{1,0:T(8,128)(2,1)}) %reduce-scatter.2.cloned.1.call-update) | async-done | bytes 589840 | tf_op jit(solution)/shard_map/reduce_scatter | solution.py:233
  272.8 2.4 add_convert_fusion
  (118 shorter events, 21.3 us)
Async XLA Ops:
  7.2 88.5 %copy-start = (bf16[3,2304,64]{1,2,0:T(8,128)(2,1)S(1)}, bf16[3,2304,64]{1,2,0:T(8,128)(2,1)}, u32[]{:S(2)}) copy-start(bf16[3,2304,64]{1,2,0:T(8,128)(2,1)} %param.13) | copy-start | bytes 2654212
  7.2 135.4 %all-gather.6.cloned.1.call-start = ((), (), s32[]{:S(2)}) async-start(), calls=%async_computation.3 | async-start | bytes 3317760 | tf_op jit(solution)/shard_map/all_gather | solution.py:159
  7.2 12.3 %collective-permute-start = (bf16[128,2304]{1,0:T(8,128)(2,1)}, bf16[128,2304]{1,0:T(8,128)(2,1)S(1)}, u32[]{:S(2)}, u32[]{:S(2)}) collective-permute-start(bf16[128,2304]{1,0:T(8,128)(2,1)} %param.10), channel_id=1, source_target_pairs={{0,1},{1,2},{2,3},{3,4},{4,5},{5,6},{6,7},{7,0},{8,9},{9,10},{10,1... | collective-permute-start | bytes 1769480 | tf_op jit(solution)/shard_map/ppermute | solution.py:131
  19.5 11.1 %collective-permute-start.1 = (bf16[128,2304]{1,0:T(8,128)(2,1)S(1)}, bf16[128,2304]{1,0:T(8,128)(2,1)S(1)}, u32[]{:S(2)}, u32[]{:S(2)}) collective-permute-start(bf16[128,2304]{1,0:T(8,128)(2,1)S(1)} %collective-permute-done), channel_id=1, source_target_pairs={{0,1},{1,2},{2,3},{3,4},{4,5},{5,6},{6,7},{7,0},{8,9},{9,10},{10,1... | collective-permute-start | bytes 1769480 | tf_op jit(solution)/shard_map/ppermute | solution.py:131
  30.7 11.1 %collective-permute-start.2 = (bf16[128,2304]{1,0:T(8,128)(2,1)S(1)}, bf16[128,2304]{1,0:T(8,128)(2,1)S(1)}, u32[]{:S(2)}, u32[]{:S(2)}) collective-permute-start(bf16[128,2304]{1,0:T(8,128)(2,1)S(1)} %collective-permute-done.1), channel_id=1, source_target_pairs={{0,1},{1,2},{2,3},{3,4},{4,5},{5,6},{6,7},{7,0},{8,9},{9,10},{10,1... | collective-permute-start | bytes 1769480 | tf_op jit(solution)/shard_map/ppermute | solution.py:131
  41.8 11.1 %collective-permute-start.3 = (bf16[128,2304]{1,0:T(8,128)(2,1)S(1)}, bf16[128,2304]{1,0:T(8,128)(2,1)S(1)}, u32[]{:S(2)}, u32[]{:S(2)}) collective-permute-start(bf16[128,2304]{1,0:T(8,128)(2,1)S(1)} %collective-permute-done.2), channel_id=1, source_target_pairs={{0,1},{1,2},{2,3},{3,4},{4,5},{5,6},{6,7},{7,0},{8,9},{9,10},{10,1... | collective-permute-start | bytes 1769480 | tf_op jit(solution)/shard_map/ppermute | solution.py:131
  52.9 0.8 copy-start.5
  53.7 11.1 %collective-permute-start.4 = (bf16[128,2304]{1,0:T(8,128)(2,1)S(1)}, bf16[128,2304]{1,0:T(8,128)(2,1)S(1)}, u32[]{:S(2)}, u32[]{:S(2)}) collective-permute-start(bf16[128,2304]{1,0:T(8,128)(2,1)S(1)} %collective-permute-done.3), channel_id=1, source_target_pairs={{0,1},{1,2},{2,3},{3,4},{4,5},{5,6},{6,7},{7,0},{8,9},{9,10},{10,1... | collective-permute-start | bytes 1769480 | tf_op jit(solution)/shard_map/ppermute | solution.py:131
  64.8 12.4 %copy-start.7 = (bf16[128,2304]{1,0:T(8,128)(2,1)}, bf16[128,2304]{1,0:T(8,128)(2,1)S(1)}, u32[]{:S(2)}) copy-start(bf16[128,2304]{1,0:T(8,128)(2,1)S(1)} %collective-permute-done.4) | copy-start | bytes 1769476
  64.8 11.2 %collective-permute-start.5 = (bf16[128,2304]{1,0:T(8,128)(2,1)S(1)}, bf16[128,2304]{1,0:T(8,128)(2,1)}, u32[]{:S(2)}, u32[]{:S(2)}) collective-permute-start(bf16[128,2304]{1,0:T(8,128)(2,1)S(1)} %collective-permute-done.4), channel_id=1, source_target_pairs={{0,1},{1,2},{2,3},{3,4},{4,5},{5,6},{6,7},{7,0},{8,9},{9,10},{10,1... | collective-permute-start | bytes 1769480 | tf_op jit(solution)/shard_map/ppermute | solution.py:131
  76.0 11.4 %collective-permute-start.6 = (bf16[128,2304]{1,0:T(8,128)(2,1)}, bf16[128,2304]{1,0:T(8,128)(2,1)}, u32[]{:S(2)}, u32[]{:S(2)}) collective-permute-start(bf16[128,2304]{1,0:T(8,128)(2,1)} %collective-permute-done.5), channel_id=1, source_target_pairs={{0,1},{1,2},{2,3},{3,4},{4,5},{5,6},{6,7},{7,0},{8,9},{9,10},{10,1... | collective-permute-start | bytes 1769480 | tf_op jit(solution)/shard_map/ppermute | solution.py:131
  78.9 13.2 %copy-start.4 = (bf16[128,2304]{1,0:T(8,128)(2,1)S(1)}, bf16[128,2304]{1,0:T(8,128)(2,1)}, u32[]{:S(2)}) copy-start(bf16[128,2304]{1,0:T(8,128)(2,1)} %param.10) | copy-start | bytes 1769476
  90.7 3.6 %copy-start.8 = (bf16[128,2304]{1,0:T(8,128)(2,1)S(1)}, bf16[128,2304]{1,0:T(8,128)(2,1)}, u32[]{:S(2)}) copy-start(bf16[128,2304]{1,0:T(8,128)(2,1)} %copy-done.7) | copy-start | bytes 1769476
  91.9 2.5 copy-start.6
  94.5 1.2 copy-start.12
  94.7 3.6 %copy-start.3 = (bf16[2048,2304]{1,0:T(8,128)(2,1)}, bf16[2048,2304]{1,0:T(8,128)(2,1)S(1)}, u32[]{:S(2)}) copy-start(bf16[2048,2304]{1,0:T(8,128)(2,1)S(1)} %constant_dynamic-update-slice_fusion) | copy-start | bytes 28311556
  103.5 6.5 %collective-permute-start.7 = (bf16[1040,128]{1,0:T(8,128)(2,1)S(1)}, bf16[1040,128]{1,0:T(8,128)(2,1)S(1)}, u32[]{:S(2)}, u32[]{:S(2)}) collective-permute-start(bf16[1040,128]{1,0:T(8,128)(2,1)S(1)} %pad_maximum_fusion.1), channel_id=1, source_target_pairs={{0,8},{8,0},{16,24},{24,16},{1,9},{9,1},{17,25},{25,17},{2,10},{10... | collective-permute-start | bytes 798728 | tf_op jit(solution)/shard_map/ppermute | solution.py:158
  105.5 9.3 %collective-permute-start.8 = (bf16[1040,128]{1,0:T(8,128)(2,1)S(1)}, bf16[1040,128]{1,0:T(8,128)(2,1)S(1)}, u32[]{:S(2)}, u32[]{:S(2)}) collective-permute-start(bf16[1040,128]{1,0:T(8,128)(2,1)S(1)} %pad_maximum_fusion.1), channel_id=1, source_target_pairs={{0,16},{8,24},{16,0},{24,8},{1,17},{9,25},{17,1},{25,9},{2,18},{10... | collective-permute-start | bytes 798728 | tf_op jit(solution)/shard_map/ppermute | solution.py:158
  107.0 11.0 %collective-permute-start.9 = (bf16[1040,128]{1,0:T(8,128)(2,1)S(1)}, bf16[1040,128]{1,0:T(8,128)(2,1)S(1)}, u32[]{:S(2)}, u32[]{:S(2)}) collective-permute-start(bf16[1040,128]{1,0:T(8,128)(2,1)S(1)} %pad_maximum_fusion.1), channel_id=1, source_target_pairs={{0,24},{8,16},{16,8},{24,0},{1,25},{9,17},{17,9},{25,1},{2,26},{10... | collective-permute-start | bytes 798728 | tf_op jit(solution)/shard_map/ppermute | solution.py:158
  107.1 58.7 %all-gather.4.cloned.1.call-start = ((), (), s32[]{:S(2)}) async-start(), calls=%async_computation.1 | async-start | bytes 1179648 | tf_op jit(solution)/shard_map/all_gather | solution.py:194
  108.5 6.3 %copy-start.10 = (s32[1024]{0:T(1024)S(1)}, s32[1024]{0:T(1024)}, u32[]{:S(2)}) copy-start(s32[1024]{0:T(1024)} %param.18) | copy-start | bytes 12292
  144.5 128.3 %reduce-scatter.2.cloned.1.call-start = ((), (), s32[]{:S(2)}) async-start(), calls=%async_computation.2 | async-start | bytes 5308416 | tf_op jit(solution)/shard_map/reduce_scatter | solution.py:233
  147.0 24.8 %copy-start.11 = (f32[2304]{0:T(1024)S(1)}, f32[2304]{0:T(1024)}, u32[]{:S(2)}) copy-start(f32[2304]{0:T(1024)} %param.12) | copy-start | bytes 27652
  171.8 3.6 %copy-start.2 = (f32[1024,2304]{1,0:T(8,128)}, f32[1024,2304]{1,0:T(8,128)S(1)}, u32[]{:S(2)}) copy-start(f32[1024,2304]{1,0:T(8,128)S(1)} %get-tuple-element.52) | copy-start | bytes 28311556
  175.5 0.9 copy-start.9
  212.6 62.5 %copy-start.1 = (bf16[3,2304,64]{1,2,0:T(8,128)(2,1)S(1)}, bf16[3,2304,64]{1,2,0:T(8,128)(2,1)}, u32[]{:S(2)}) copy-start(bf16[3,2304,64]{1,2,0:T(8,128)(2,1)} %param.13) | copy-start | bytes 2654212
Sparse Core Ops, SparseCore 0:
  107.2 35.3 all-gather.5
  144.8 20.9 all-gather.3
  218.2 54.5 reduce-scatter.1
